TPU v7x, 256 devices: a whole 4x4x8 slice. The times are simulated.
256 devices in a mesh: section: 32 (over y, x, z_lo), tensor: 8 (over z_hi, core).
Axes of the slice: x: 4, y: 4, z: 8 (z_hi: 4, z_lo: 2; z = z_hi * 2 + z_lo), core: 2. Of those that a mesh axis runs over, the one named last changes fastest.
Arguments:
- layer_input: bfloat16 [32, 2, 256, 3072], P('section', None, None, 'tensor'), may hold values from -6 to 6
- upstream: bfloat16 [32, 2, 256, 3072], P('section', None, None, 'tensor'), may hold values from -6 to 6
- scores: bfloat16 [32, 2, 16, 256, 256], P('section', None, 'tensor'), may hold values from -12 to 260, as said below
- value_weight: bfloat16 [32, 3072, 2048], P('section', None, 'tensor'), may hold values from -0.109375 to 0.109375
- out_weight: bfloat16 [32, 2048, 3072], P('section', 'tensor'), may hold values from -0.125 to 0.125
- feedback: float32 [32, 2, 256, 3072], P('section', None, None, 'tensor'), may hold values from -4 to 4
- basis: float32 [3072, 128], P('tensor'), may hold values from -0.3125 to 0.3125
Outputs:
- grad_out_weight: bfloat16 [32, 2048, 3072], P('section', 'tensor')
- grad_value_weight: bfloat16 [32, 3072, 2048], P('section', None, 'tensor')
- new_feedback: float32 [32, 2, 256, 3072], P('section', None, None, 'tensor')
- rebuilt: bfloat16 [32, 2, 256, 3072], P('section', None, None, 'tensor')
Inputs may be any that keep to these rules, and one draw needn't show every extreme that they name: `scores`: only entries with key position at or before the query position are read.
All inputs are finite; a program needn't handle non-finite values.
Results may differ from a plain program's by a relative error of at most 0.015.
Values may be sent and summed in bfloat16 or wider, within the bound.
A program may use at most 64 MiB of HBM per device.

v0:
```python
import jax
import jax.numpy as jnp
from jax import lax
from jax.sharding import PartitionSpec as P


def from_behind(value, axis, steps):
    count = lax.axis_size(axis)
    initial, last = (max(0, -steps), min(count, count - steps))
    return lax.ppermute(value, axis, [(source, source + steps) for source in range(initial, last)])


def causal_probs(raw_scores):
    length = raw_scores.shape[-1]
    row_ids = lax.broadcasted_iota(jnp.int32, (length, length), 0)
    col_ids = lax.broadcasted_iota(jnp.int32, (length, length), 1)
    causal = col_ids <= row_ids
    raised = jnp.where(causal, raw_scores.astype(jnp.float32), -1e30)
    largest = jnp.max(raised, axis=-1, keepdims=True)
    powers = jnp.where(causal, jnp.exp(raised - largest), 0.0)
    return (powers / jnp.sum(powers, axis=-1, keepdims=True)).astype(jnp.bfloat16)


def on_device(layer_input, upstream, scores, value_weight, out_weight, feedback, basis):
    micro_count = layer_input.shape[1]
    length = layer_input.shape[2]
    shard_width = layer_input.shape[3]
    row_count = micro_count * length
    local_heads = scores.shape[2]
    inner_width = out_weight.shape[1]
    head_size = inner_width // local_heads
    full_input, full_grad = (
        lax.all_gather(layer_input[0], "tensor", axis=2, tiled=True),
        lax.all_gather(upstream[0], "tensor", axis=2, tiled=True),
    )
    model_width = full_input.shape[2]
    flat_input = full_input.reshape(row_count, model_width)
    flat_grad = full_grad.reshape(row_count, model_width)
    weight_value = value_weight[0]
    weight_out = out_weight[0]
    value_act = jnp.dot(flat_input, weight_value, preferred_element_type=jnp.float32).astype(
        jnp.bfloat16
    )
    value_act = value_act.reshape(micro_count, length, local_heads, head_size)
    attention = causal_probs(scores[0])
    attended = jnp.einsum(
        "bhqk,bkhd->bqhd", attention, value_act, preferred_element_type=jnp.float32
    )
    attended = attended.astype(jnp.bfloat16).reshape(row_count, inner_width)
    attended_grad = jnp.dot(flat_grad, weight_out.T, preferred_element_type=jnp.float32).astype(
        jnp.bfloat16
    )
    grad_out_weight = jnp.dot(attended.T, flat_grad, preferred_element_type=jnp.float32).astype(
        jnp.bfloat16
    )
    value_grad = jnp.einsum(
        "bhqk,bqhd->bkhd",
        attention,
        attended_grad.reshape(micro_count, length, local_heads, head_size),
        preferred_element_type=jnp.float32,
    )
    value_grad = value_grad.astype(jnp.bfloat16).reshape(row_count, inner_width)
    grad_value_weight = jnp.dot(
        flat_input.T, value_grad, preferred_element_type=jnp.float32
    ).astype(jnp.bfloat16)
    own_grad = upstream[0].reshape(row_count, shard_width).astype(jnp.float32)
    partial_terms = jnp.dot(value_grad, weight_value.T, preferred_element_type=jnp.float32)
    through = lax.psum_scatter(partial_terms, "tensor", scatter_dimension=1, tiled=True)
    carried = own_grad + through + feedback[0].reshape(row_count, shard_width)
    factors = jnp.dot(
        carried, basis, precision=lax.Precision.HIGHEST, preferred_element_type=jnp.float32
    ).astype(jnp.bfloat16)
    new_feedback = carried - jnp.dot(
        factors.astype(jnp.float32), basis.T, precision=lax.Precision.HIGHEST
    )
    arrived = from_behind(factors, "section", -1)
    rebuilt = jnp.dot(arrived.astype(jnp.float32), basis.T, precision=lax.Precision.HIGHEST).astype(
        jnp.bfloat16
    )
    return (
        grad_out_weight[None],
        grad_value_weight[None],
        new_feedback.reshape(1, micro_count, length, shard_width),
        rebuilt.reshape(1, micro_count, length, shard_width),
    )


def solution(mesh):
    in_specs = (
        P("section", None, None, "tensor"),
        P("section", None, None, "tensor"),
        P("section", None, "tensor", None, None),
        P("section", None, "tensor"),
        P("section", "tensor", None),
        P("section", None, None, "tensor"),
        P("tensor", None),
    )
    out_specs = (
        P("section", "tensor", None),
        P("section", None, "tensor"),
        P("section", None, None, "tensor"),
        P("section", None, None, "tensor"),
    )
    return jax.shard_map(
        on_device, mesh=mesh, in_specs=in_specs, out_specs=out_specs, check_vma=False
    )
```

profile of v0, /device:TPU:6, one launch (start us, length us, event | category | flops | bytes accessed | tf_op | source)
XLA Modules:
  0.0 199.5 jit_solution(15959721739184531660)
XLA Ops:
  7.2 0.0 copy-start
  7.2 0.0 all-gather.7.cloned.1.call-start
  7.2 0.7 all-gather.7.cloned.1.call-update
  7.9 0.0 all-gather.5.cloned.1.call-start
  8.0 0.7 all-gather.5.cloned.1.call-update
  8.7 0.0 reduce-scatter.2.cloned.1.call-start
  8.7 1.9 fusion.34
  10.6 46.5 %all-gather.7.cloned.1.call-done = bf16[1,2,256,3072]{3,2,1,0:T(8,128)(2,1)} async-done(((bf16[1,2,256,384]{3,2,1,0:T(8,128)(2,1)}), bf16[1,2,256,3072]{3,2,1,0:T(8,128)(2,1)}) %all-gather.7.cloned.1.call-update) | async-done | bytes 3145744 | tf_op jit(solution)/shard_map/all_gather | solution.py:34
  57.1 3.4 %fusion.15 = bf16[512,256]{1,0:T(8,128)(2,1)S(1)} fusion(bf16[512,3072]{1,0:T(8,128)(2,1)} %bitcast.72, bf16[1,256,3072]{2,1,0:T(8,128)(2,1)} %param.11), kind=kOutput, calls=%fused_computation.17 | convolution fusion | flops 805437440 | bytes 4980736 | tf_op jit(solution)/shard_map/dot_general | solution.py:50
  60.5 0.1 reshape.42
  60.6 3.4 %fusion.19 = bf16[2,256,2,128]{1,3,2,0:T(8,128)(2,1)S(1)} fusion(bf16[2,256,2,128]{3,2,1,0:T(2,128)(2,1)S(1)} %reshape.42, f32[2,2,256]{2,1,0:T(2,128)S(1)} %fusion.34, bf16[1,2,2,256,256]{4,3,2,1,0:T(8,128)(2,1)} %param.9, pred[256,256]{1,0:T(8,128)(4,1)S(1)} %iota_compare_fusion), kind=kOutput, calls=%fused_computation.21 | convolution fusion | flops 68814080 | bytes 1118208 | tf_op jit(solution)/shard_map/bhqk,bqhd->bkhd/dot_general | solution.py:56
  64.0 0.2 copy.17
  64.2 0.0 copy-done
  64.2 3.7 %fusion.5 = f32[512,3072]{1,0:T(8,128)} fusion(bf16[1,3072,256]{2,1,0:T(8,128)(2,1)S(1)} %copy-done, bf16[64,8,2,128]{3,2,1,0:T(2,128)(2,1)S(1)} %bitcast.70), kind=kOutput, calls=%fused_computation.7 | convolution fusion | flops 805306368 | bytes 8126464 | tf_op jit(solution)/shard_map/dot_general | solution.py:67
  67.8 0.0 reduce-scatter.2.cloned.1.call-update
  67.9 33.6 %all-gather.5.cloned.1.call-done = bf16[1,2,256,3072]{3,2,1,0:T(8,128)(2,1)} async-done(((bf16[1,2,256,384]{3,2,1,0:T(8,128)(2,1)}), bf16[1,2,256,3072]{3,2,1,0:T(8,128)(2,1)}) %all-gather.5.cloned.1.call-update) | async-done | bytes 3145744 | tf_op jit(solution)/shard_map/all_gather | solution.py:33
  101.5 2.9 %fusion.2 = bf16[1,3072,256]{1,2,0:T(8,128)(2,1)S(1)} fusion(bf16[512,3072]{1,0:T(8,128)(2,1)} %bitcast.74, bf16[64,8,2,128]{3,2,1,0:T(2,128)(2,1)S(1)} %bitcast.71), kind=kOutput, calls=%fused_computation.4 | convolution fusion | flops 806092800 | bytes 4980736 | tf_op jit(solution)/shard_map/dot_general | solution.py:63
  104.4 1.6 copy.18
  106.0 2.9 %fusion.12 = bf16[512,256]{1,0:T(8,128)(2,1)S(1)} fusion(bf16[512,3072]{1,0:T(8,128)(2,1)} %bitcast.75, bf16[1,3072,256]{2,1,0:T(8,128)(2,1)S(1)} %copy-done), kind=kOutput, calls=%fused_computation.16 | convolution fusion | flops 805437440 | bytes 4980736 | tf_op jit(solution)/shard_map/dot_general | solution.py:41
  108.8 0.1 reshape.39
  108.9 3.4 %fusion.18 = bf16[2,256,2,128]{1,3,2,0:T(8,128)(2,1)S(1)} fusion(bf16[2,256,2,128]{3,2,1,0:T(2,128)(2,1)S(1)} %reshape.39, f32[2,2,256]{2,1,0:T(2,128)S(1)} %fusion.34, bf16[1,2,2,256,256]{4,3,2,1,0:T(8,128)(2,1)} %param.9, pred[256,256]{1,0:T(8,128)(4,1)S(1)} %iota_compare_fusion), kind=kOutput, calls=%fused_computation.20 | convolution fusion | flops 68814080 | bytes 1118208 | tf_op jit(solution)/shard_map/bhqk,bkhd->bqhd/dot_general | solution.py:46
  112.4 0.0 copy-start.2
  112.4 0.0 copy-start.3
  112.4 0.2 copy.15
  112.6 0.0 copy-start.1
  112.6 4.7 %fusion.1 = bf16[1,256,3072]{2,1,0:T(8,128)(2,1)} fusion(bf16[512,3072]{1,0:T(8,128)(2,1)} %bitcast.73, bf16[64,8,2,128]{3,2,1,0:T(2,128)(2,1)S(1)} %bitcast.76), kind=kOutput, calls=%fused_computation.3 | convolution fusion | flops 806092800 | bytes 4980736 | tf_op jit(solution)/shard_map/dot_general | solution.py:53
  117.3 65.5 %reduce-scatter.2.cloned.1.call-done = f32[512,384]{1,0:T(8,128)} async-done(((f32[512,3072]{1,0:T(8,128)}), f32[512,384]{1,0:T(8,128)}) %reduce-scatter.2.cloned.1.call-update) | async-done | bytes 786448 | tf_op jit(solution)/shard_map/reduce_scatter | solution.py:68
  182.8 0.0 copy-done.2
  182.8 0.0 copy-done.3
  182.8 1.2 fusion.21
  184.0 0.0 copy-done.1
  184.1 0.8 convolution_convert_fusion.5
  184.9 1.9 collective-permute-start
  186.8 1.4 convolution_subtract_fusion
  188.1 3.6 %collective-permute-done = bf16[512,128]{1,0:T(8,128)(2,1)S(1)} collective-permute-done((bf16[512,128]{1,0:T(8,128)(2,1)S(1)}, bf16[512,128]{1,0:T(8,128)(2,1)S(1)}, u32[]{:S(2)}, u32[]{:S(2)}) %collective-permute-start) | collective-permute-done | bytes 131104 | tf_op jit(solution)/shard_map/ppermute | solution.py:10
  191.7 1.2 convolution_convert_fusion.2
  (1 shorter events, 0.0 us)
Async XLA Ops:
  7.2 57.0 %copy-start = (bf16[1,3072,256]{2,1,0:T(8,128)(2,1)S(1)}, bf16[1,3072,256]{2,1,0:T(8,128)(2,1)}, u32[]{:S(2)}) copy-start(bf16[1,3072,256]{2,1,0:T(8,128)(2,1)} %param.10) | copy-start | bytes 4718596
  7.2 49.9 %all-gather.7.cloned.1.call-start = ((), (), s32[]{:S(2)}) async-start(), calls=%async_computation.3 | async-start | bytes 3538944 | tf_op jit(solution)/shard_map/all_gather | solution.py:34
  7.9 93.6 %all-gather.5.cloned.1.call-start = ((), (), s32[]{:S(2)}) async-start(), calls=%async_computation.2 | async-start | bytes 3538944 | tf_op jit(solution)/shard_map/all_gather | solution.py:33
  8.7 174.1 %reduce-scatter.2.cloned.1.call-start = ((), (), s32[]{:S(2)}) async-start(), calls=%async_computation.1 | async-start | bytes 7077888 | tf_op jit(solution)/shard_map/reduce_scatter | solution.py:68
  112.4 70.5 %copy-start.2 = (bf16[1,2,256,384]{3,2,1,0:T(8,128)(2,1)S(1)}, bf16[1,2,256,384]{3,2,1,0:T(8,128)(2,1)}, u32[]{:S(2)}) copy-start(bf16[1,2,256,384]{3,2,1,0:T(8,128)(2,1)} %param.8) | copy-start | bytes 1179652
  112.4 70.4 %copy-start.3 = (f32[1,2,256,384]{3,2,1,0:T(8,128)S(1)}, f32[1,2,256,384]{3,2,1,0:T(8,128)}, u32[]{:S(2)}) copy-start(f32[1,2,256,384]{3,2,1,0:T(8,128)} %param.12) | copy-start | bytes 2359300
  112.6 71.5 %copy-start.1 = (f32[384,128]{1,0:T(8,128)S(1)}, f32[384,128]{1,0:T(8,128)}, u32[]{:S(2)}) copy-start(f32[384,128]{1,0:T(8,128)} %param.13) | copy-start | bytes 589828
  184.9 6.9 %collective-permute-start = (bf16[512,128]{1,0:T(8,128)(2,1)S(1)}, bf16[512,128]{1,0:T(8,128)(2,1)S(1)}, u32[]{:S(2)}, u32[]{:S(2)}) collective-permute-start(bf16[512,128]{1,0:T(8,128)(2,1)S(1)} %convolution_convert_fusion.5), channel_id=1, source_target_pairs={{8,0},{16,8},{24,16},{32,24},{40,32},{48,40},{56,48},{64,56},{72,6... | collective-permute-start | bytes 393224 | tf_op jit(solution)/shard_map/ppermute | solution.py:10
Sparse Core Ops, SparseCore 0:
  9.9 47.2 all-gather.6
  58.9 42.5 all-gather.4
  104.1 78.6 reduce-scatter.1
where the time goes:
time: 200 us; the launch traced here: 199 us
  waiting for transfers between devices  151 us (76%)
  matrix products  27.8 us (14%)
  between operations  13.9 us (7%)
  other arithmetic  3.13 us (2%)
  local copies, waits for them, and re-layouts  2.06 us (1%)
  starting transfers between devices  2.03 us (1%)
    reduce_scatter x1, waiting for transfers between devices, on_device(): lax.psum_scatter(partial_terms, 'tensor', scatter_dimension=1, tiled=True)  65.5 us
    all_gather x1, waiting for transfers between devices, on_device(): lax.all_gather(upstream[0], 'tensor', axis=2, tiled=True)  46.5 us
    all_gather x1, waiting for transfers between devices, on_device(): lax.all_gather(layer_input[0], 'tensor', axis=2, tiled=True)  33.6 us
    dot_general x1, matrix products, on_device(): jnp.dot(attended.T, flat_grad, preferred_element_type=jnp.float32)  4.71 us
  transfers between devices with their start and end apart: 4, of which 4 were waited for; matrix products, arithmetic and copies ran while one was open for 15% of the time, Pallas kernels for 0%

commit v1 on v0

v1 whole, which is shorter than its diff:
```python
import functools

import jax
import jax.numpy as jnp
from jax import lax
from jax.experimental import pallas as pl
from jax.experimental.pallas import tpu as pltpu
from jax.sharding import PartitionSpec as P

MESH = pl.DeviceIdType.MESH
NT = (((1,), (1,)), ((), ()))
TN = (((0,), (0,)), ((), ()))
F32 = jnp.float32
BF16 = jnp.bfloat16


def dot(a, b, dims=(((1,), (0,)), ((), ()))):
    return lax.dot_general(a, b, dims, preferred_element_type=F32)


def halves(value):
    high = value.astype(BF16)
    return high, (value - high.astype(F32)).astype(BF16)


def body(
    micro, heads, n_section,
    x_hbm, u_hbm, scores_hbm, wv_hbm, wo_hbm, feedback_hbm, basis_hbm,
    gow_hbm, gvw_hbm, new_hbm, rebuilt_hbm,
    u, x, wv, wo, wv_far, scores, feedback, basis,
    att, att_t, sums, vg, vg_far, parts, out_stage, in_hop, in_left, in_right,
    factors, factors_in, gow, gvw, new, rebuilt,
    load_sem, send_sem, recv_sem, store_sem,
):
    rows, width = u_hbm.shape
    half = rows // 2
    length = rows // micro
    inner = wv_hbm.shape[1]
    head = inner // heads

    s = lax.axis_index("section")
    t = lax.axis_index("tensor")
    chip, core = t // 2, lax.rem(t, 2)

    def place(step, which):
        return lax.rem(chip + step, 4) * 2 + which

    right = (s, place(1, core))
    left = (s, place(3, core))
    sister = (s, place(0, 1 - core))
    behind = (lax.rem(s + n_section - 1, n_section), t)
    ahead = (lax.rem(s + 1, n_section), t)

    owner = [place(step, which) for which in (core, 1 - core) for step in (0, 3, 1, 2)]

    def block_of(slot):
        return pl.ds(pl.multiple_of(owner[slot] * width, 128), width)

    lo, hi = pl.ds(0, half), pl.ds(half, half)

    loads = []

    def load(src, dst):
        copy = pltpu.make_async_copy(src, dst, load_sem.at[len(loads)])
        copy.start()
        loads.append(copy)
        return copy

    got_scores = load(scores_hbm, scores)
    got_u = load(u_hbm, u.at[0])
    got_wo = load(wo_hbm, wo)
    got_wv = load(wv_hbm, wv)
    got_x = load(x_hbm, x.at[0])
    got_feedback = load(feedback_hbm, feedback)
    got_basis = load(basis_hbm, basis)

    barrier = pltpu.get_barrier_semaphore()
    peers = (right, left, sister, behind, ahead)
    for peer in peers:
        pl.semaphore_signal(barrier, inc=1, device_id=peer, device_id_type=MESH)
    pl.semaphore_wait(barrier, len(peers))

    sent = []

    def send(src, dst, device):
        i = len(sent)
        copy = pltpu.make_async_remote_copy(
            src_ref=src, dst_ref=dst, send_sem=send_sem.at[i], recv_sem=recv_sem.at[i],
            device_id=device, device_id_type=MESH,
        )
        copy.start()
        sent.append(copy)
        return copy

    u1lo = send(u_hbm.at[lo], u.at[1, lo], right)
    u2hi = send(u_hbm.at[hi], u.at[2, hi], left)
    u1hi = send(u_hbm.at[hi], u.at[1, hi], right)
    u2lo = send(u_hbm.at[lo], u.at[2, lo], left)
    u4 = send(u_hbm, u.at[4], sister)
    far = []
    for step in range(4):
        block = pl.ds(pl.multiple_of(place(step, 1 - core) * width, 128), width)
        far.append(send(wv_hbm.at[block], wv_far.at[step], sister))

    got_scores.wait()
    query = lax.broadcasted_iota(jnp.int32, (length, length), 0)
    key = lax.broadcasted_iota(jnp.int32, (length, length), 1)
    causal = key <= query
    for i in range(micro * heads):
        raised = jnp.where(causal, scores[i].astype(F32), -1e30)
        largest = jnp.max(raised, axis=-1, keepdims=True)
        powers = jnp.where(causal, jnp.exp(raised - largest), 0.0)
        probs = powers / jnp.sum(powers, axis=-1, keepdims=True)
        att[i] = probs.astype(BF16)
        att_t[i] = probs.T.astype(BF16)

    def add_u(slot, first=False):
        term = dot(u[slot], wo[:, block_of(slot)], NT)
        sums[...] = term if first else sums[...] + term

    got_u.wait()
    got_wo.wait()
    add_u(0, True)

    u1lo.wait_recv()
    u3lo = send(u.at[1, lo], u.at[3, lo], right)
    u5lo = send(u.at[1, lo], u.at[5, lo], sister)
    u2hi.wait_recv()
    u3hi = send(u.at[2, hi], u.at[3, hi], left)
    u6hi = send(u.at[2, hi], u.at[6, hi], sister)
    u4.wait_recv()
    add_u(4)
    u1hi.wait_recv()
    u5hi = send(u.at[1, hi], u.at[5, hi], sister)
    u2lo.wait_recv()
    u6lo = send(u.at[2, lo], u.at[6, lo], sister)

    x1lo = send(x_hbm.at[lo], x.at[1, lo], right)
    x2hi = send(x_hbm.at[hi], x.at[2, hi], left)
    x4 = send(x_hbm, x.at[4], sister)

    add_u(1)
    add_u(2)
    u5lo.wait_recv()
    u5hi.wait_recv()
    add_u(5)
    u6lo.wait_recv()
    u6hi.wait_recv()
    add_u(6)
    u3lo.wait_recv()
    u7lo = send(u.at[3, lo], u.at[7, lo], sister)
    u3hi.wait_recv()
    u7hi = send(u.at[3, hi], u.at[7, hi], sister)
    add_u(3)
    u7lo.wait_recv()
    u7hi.wait_recv()
    add_u(7)

    x1hi = send(x_hbm.at[hi], x.at[1, hi], right)
    x2lo = send(x_hbm.at[lo], x.at[2, lo], left)

    for b in range(micro):
        for h in range(heads):
            at_rows, at_columns = pl.ds(b * length, length), pl.ds(h * head, head)
            grad = dot(att_t[b * heads + h], sums[at_rows, at_columns].astype(BF16))
            vg[at_rows, at_columns] = grad.astype(BF16)
    vg_copy = send(vg, vg_far, sister)

    got_wv.wait()

    def partial(step):
        block = pl.ds(pl.multiple_of(place(step, core) * width, 128), width)
        near = dot(vg[...], wv[block, :], NT)
        return near, wv_far.at[step]

    near, _ = partial(2)
    parts[2] = near
    for copy in far:
        copy.wait_recv()
    vg_copy.wait_recv()
    out_stage[0] = (parts[2] + dot(vg_far[...], wv_far[2], NT)).astype(BF16).reshape(2, half, width)
    hop_right = send(out_stage.at[0, 0], in_hop.at[0], right)
    hop_left = send(out_stage.at[0, 1], in_hop.at[1], left)
    for step in (1, 3, 0):
        near, weight = partial(step)
        parts[step] = near + dot(vg_far[...], weight[...], NT)
        if step == 1:
            out_stage[1, 1] = parts[1, half:].astype(BF16)
            last_right_hi = send(out_stage.at[1, 1], in_left.at[1], right)
        if step == 3:
            out_stage[2, 0] = parts[3, :half].astype(BF16)
            last_left_lo = send(out_stage.at[2, 0], in_right.at[0], left)

    def add_x(slot, first=False):
        term = dot(x[slot], wv[block_of(slot), :])
        sums[...] = term if first else sums[...] + term

    stores = []

    def store(src, dst):
        copy = pltpu.make_async_copy(src, dst, store_sem.at[len(stores)])
        copy.start()
        stores.append(copy)

    def grad_value(slot):
        gvw[slot] = dot(x[slot], vg[...], TN).astype(BF16)
        store(gvw.at[slot], gvw_hbm.at[block_of(slot)])

    def take_x(slot, first=False):
        add_x(slot, first)
        grad_value(slot)

    got_x.wait()
    take_x(0, True)

    x1lo.wait_recv()
    x3lo = send(x.at[1, lo], x.at[3, lo], right)
    x5lo = send(x.at[1, lo], x.at[5, lo], sister)
    x2hi.wait_recv()
    x3hi = send(x.at[2, hi], x.at[3, hi], left)
    x6hi = send(x.at[2, hi], x.at[6, hi], sister)

    hop_right.wait_recv()
    out_stage[1, 0] = (parts[1, :half] + in_hop[0].astype(F32)).astype(BF16)
    last_right_lo = send(out_stage.at[1, 0], in_left.at[0], right)
    hop_left.wait_recv()
    out_stage[2, 1] = (parts[3, half:] + in_hop[1].astype(F32)).astype(BF16)
    last_left_hi = send(out_stage.at[2, 1], in_right.at[1], left)

    x4.wait_recv()
    take_x(4)

    x1hi.wait_recv()
    x5hi = send(x.at[1, hi], x.at[5, hi], sister)
    x2lo.wait_recv()
    x6lo = send(x.at[2, lo], x.at[6, lo], sister)
    take_x(1)
    take_x(2)
    x5lo.wait_recv()
    x5hi.wait_recv()
    take_x(5)
    x6lo.wait_recv()
    x6hi.wait_recv()
    take_x(6)

    got_feedback.wait()
    got_basis.wait()
    basis_high, basis_low = halves(basis[...])
    feedback[...] += u[0].astype(F32) + parts[0]
    last_right_lo.wait_recv()
    last_right_hi.wait_recv()
    last_left_lo.wait_recv()
    last_left_hi.wait_recv()
    carried = feedback[...] + in_left[...].astype(F32).reshape(rows, width)
    carried = carried + in_right[...].astype(F32).reshape(rows, width)
    high, low = halves(carried)
    factors[...] = (dot(high, basis_high) + dot(low, basis_high) + dot(high, basis_low)).astype(BF16)
    factor_copy = send(factors, factors_in, behind)
    own = factors[...]
    new[...] = carried - (dot(own, basis_high, NT) + dot(own, basis_low, NT))
    store(new, new_hbm)

    x3lo.wait_recv()
    x7lo = send(x.at[3, lo], x.at[7, lo], sister)
    x3hi.wait_recv()
    x7hi = send(x.at[3, hi], x.at[7, hi], sister)
    take_x(3)

    factor_copy.wait_recv()
    arrived = factors_in[...]
    built = dot(arrived, basis_high, NT) + dot(arrived, basis_low, NT)
    rebuilt[...] = jnp.where(s == n_section - 1, 0.0, built).astype(BF16)
    store(rebuilt, rebuilt_hbm)

    x7lo.wait_recv()
    x7hi.wait_recv()
    take_x(7)

    for b in range(micro):
        for h in range(heads):
            at_rows, at_columns = pl.ds(b * length, length), pl.ds(h * head, head)
            value = dot(att[b * heads + h], sums[at_rows, at_columns].astype(BF16))
            vg_far[at_rows, at_columns] = value.astype(BF16)
    attended = vg_far[...]
    for slot in range(8):
        gow[slot] = dot(attended, u[slot], TN).astype(BF16)
        store(gow.at[slot], gow_hbm.at[:, block_of(slot)])

    for copy in stores:
        copy.wait()
    for copy in sent:
        copy.wait_send()


def on_device(n_section, layer_input, upstream, scores, value_weight, out_weight, feedback, basis):
    _, micro, length, width = layer_input.shape
    rows, half = micro * length, micro * length // 2
    heads = scores.shape[2]
    model, inner = value_weight.shape[1:]
    rank = basis.shape[1]
    vmem = pltpu.VMEM
    anywhere = pl.BlockSpec(memory_space=pl.ANY)
    gow, gvw, new, rebuilt = pl.pallas_call(
        functools.partial(body, micro, heads, n_section),
        out_shape=(
            jax.ShapeDtypeStruct((inner, model), BF16),
            jax.ShapeDtypeStruct((model, inner), BF16),
            jax.ShapeDtypeStruct((rows, width), F32),
            jax.ShapeDtypeStruct((rows, width), BF16),
        ),
        in_specs=[anywhere] * 7,
        out_specs=(anywhere,) * 4,
        scratch_shapes=[
            vmem((8, rows, width), BF16),
            vmem((8, rows, width), BF16),
            vmem((model, inner), BF16),
            vmem((inner, model), BF16),
            vmem((4, width, inner), BF16),
            vmem((micro * heads, length, length), BF16),
            vmem((rows, width), F32),
            vmem((width, rank), F32),
            vmem((micro * heads, length, length), BF16),
            vmem((micro * heads, length, length), BF16),
            vmem((rows, inner), F32),
            vmem((rows, inner), BF16),
            vmem((rows, inner), BF16),
            vmem((4, rows, width), F32),
            vmem((3, 2, half, width), BF16),
            vmem((2, half, width), BF16),
            vmem((2, half, width), BF16),
            vmem((2, half, width), BF16),
            vmem((rows, rank), BF16),
            vmem((rows, rank), BF16),
            vmem((8, inner, width), BF16),
            vmem((8, width, inner), BF16),
            vmem((rows, width), F32),
            vmem((rows, width), BF16),
            pltpu.SemaphoreType.DMA((7,)),
            pltpu.SemaphoreType.DMA((40,)),
            pltpu.SemaphoreType.DMA((40,)),
            pltpu.SemaphoreType.DMA((18,)),
        ],
        compiler_params=pltpu.CompilerParams(
            collective_id=0, has_side_effects=True, vmem_limit_bytes=56 << 20
        ),
    )(
        layer_input.reshape(rows, width),
        upstream.reshape(rows, width),
        scores.reshape(micro * heads, length, length),
        value_weight[0],
        out_weight[0],
        feedback.reshape(rows, width),
        basis,
    )
    shape = (1, micro, length, width)
    return gow[None], gvw[None], new.reshape(shape), rebuilt.reshape(shape)


def solution(mesh):
    in_specs = (
        P("section", None, None, "tensor"),
        P("section", None, None, "tensor"),
        P("section", None, "tensor", None, None),
        P("section", None, "tensor"),
        P("section", "tensor", None),
        P("section", None, None, "tensor"),
        P("tensor", None),
    )
    out_specs = (
        P("section", "tensor", None),
        P("section", None, "tensor"),
        P("section", None, None, "tensor"),
        P("section", None, None, "tensor"),
    )
    return jax.shard_map(
        functools.partial(on_device, mesh.shape["section"]),
        mesh=mesh, in_specs=in_specs, out_specs=out_specs, check_vma=False,
    )
```

time: 200 us -> 103 us (0.52)
  waiting for transfers between devices: 151 us -> 0 us
  Pallas kernels: 0 us -> 95.5 us
  matrix products: 27.8 us -> 0 us
  between operations: 13.9 us -> 0.65 us
  local copies, waits for them, and re-layouts: 2.06 us -> 6.08 us
  other arithmetic: 3.13 us -> 0 us
  starting transfers between devices: 2.03 us -> 0 us
    pallas_call x0 -> x1, Pallas kernels: none -> 95.5 us  [on_device(): pl.pallas_call(functools.partial(body, micro, heads, n_section), out_shap...]
    all_gather x2 -> x0, waiting for transfers between devices: 80.1 us -> none  [the longest x1 46.5 us: on_device(): lax.all_gather(upstream[0], 'tensor', axis=2, tiled=True)]
    reduce_scatter x1 -> x0, waiting for transfers between devices: 65.5 us -> none  [on_device(): lax.psum_scatter(partial_terms, 'tensor', scatter_dimension=1, tiled=True)]
    dot_general x10 -> x0, matrix products: 27.8 us -> none  [the longest x1 4.71 us: on_device(): jnp.dot(attended.T, flat_grad, preferred_element_type=jnp.float32)]
    unnamed x9 -> x10, local copies, waits for them, and re-layouts: 1.59 us -> 6.08 us
    ppermute x1 -> x0, waiting for transfers between devices: 3.57 us -> none  [from_behind(): lax.ppermute(value, axis, [(source, source + steps) for source in range(i...]
  transfers between devices with their start and end apart: 4 -> 0, of which waited for: 4 -> 0; matrix products, arithmetic and copies ran while one was open for 15% -> 0% of each run, Pallas kernels for 0% -> 0%
where the time goes in v1:
time: 103 us; the launch traced here: 102 us
  Pallas kernels  95.5 us (93%)
  local copies, waits for them, and re-layouts  6.08 us (6%)
    pallas_call x1, Pallas kernels, on_device(): pl.pallas_call(functools.partial(body, micro, heads, n_section), out_shap...  95.5 us
    unnamed x10, local copies, waits for them, and re-layouts  6.08 us

profile of v1, /device:TPU:6, one launch (start us, length us, event | category | flops | bytes accessed | tf_op | source)
XLA Modules:
  0.0 102.2 jit_solution(4135802364154489581)
XLA Ops:
  0.6 95.5 %shard_map.102 = (bf16[256,3072]{1,0:T(8,128)(2,1)}, bf16[3072,256]{1,0:T(8,128)(2,1)}, f32[512,384]{1,0:T(8,128)}, bf16[512,384]{1,0:T(8,128)(2,1)}) custom-call(bf16[512,384]{1,0:T(8,128)(2,1)} %bitcast.18, bf16[512,384]{1,0:T(8,128)(2,1)} %bitcast.19, bf16[4,256,256]{2,1,0:T(8,128)(2,1)} %bitcast.16, bf16[3072,256]{1,0:T(8,128)(2,1)} %bitcast.12, ...), custom_call_target="tpu_custom_call" | custom-call | tf_op jit(solution)/shard_map/pallas_call | solution.py:303
  96.1 0.0 copy-start
  96.1 2.8 %copy.15 = bf16[1,256,3072]{2,1,0:T(8,128)(2,1)} copy(bf16[1,256,3072]{2,1,0:T(8,128)(2,1)} %bitcast.11) | data formatting | bytes 3145728
  98.9 0.0 copy-done
  98.9 0.0 copy-start.1
  98.9 0.0 copy-start.2
  98.9 1.1 %copy.16 = bf16[1,3072,256]{2,1,0:T(8,128)(2,1)} copy(bf16[1,3072,256]{2,1,0:T(8,128)(2,1)S(1)} %bitcast.10) | data formatting | bytes 3145728
  100.1 0.5 copy-done.1
  100.6 0.9 copy.17
  101.5 0.0 copy-done.2
  101.5 0.7 copy.18
Async XLA Ops:
  96.1 2.8 %copy-start = (bf16[3072,256]{1,0:T(8,128)(2,1)S(1)}, bf16[3072,256]{1,0:T(8,128)(2,1)}, u32[]{:S(2)}) copy-start(bf16[3072,256]{1,0:T(8,128)(2,1)} %get-tuple-element.9) | copy-start | bytes 4718596
  98.9 1.7 %copy-start.1 = (f32[512,384]{1,0:T(8,128)S(1)}, f32[512,384]{1,0:T(8,128)}, u32[]{:S(2)}) copy-start(f32[512,384]{1,0:T(8,128)} %get-tuple-element.10) | copy-start | bytes 2359300
  98.9 2.6 %copy-start.2 = (bf16[512,384]{1,0:T(8,128)(2,1)S(1)}, bf16[512,384]{1,0:T(8,128)(2,1)}, u32[]{:S(2)}) copy-start(bf16[512,384]{1,0:T(8,128)(2,1)} %get-tuple-element.11) | copy-start | bytes 1179652

commit v2 on v1

--- a/solution.py
+++ b/solution.py
@@ -23,14 +23,21 @@
     return high, (value - high.astype(F32)).astype(BF16)
 
 
+def blocks(chip, core, width):
+    owner = [
+        lax.rem(chip + step, 4) * 2 + which for which in (core, 1 - core) for step in (0, 3, 1, 2)
+    ]
+    return lambda slot: pl.ds(pl.multiple_of(owner[slot] * width, 128), width)
+
+
 def body(
     micro, heads, n_section,
     x_hbm, u_hbm, scores_hbm, wv_hbm, wo_hbm, feedback_hbm, basis_hbm,
-    gow_hbm, gvw_hbm, new_hbm, rebuilt_hbm,
-    u, x, wv, wo, wv_far, scores, feedback, basis,
-    att, att_t, sums, vg, vg_far, parts, out_stage, in_hop, in_left, in_right,
-    factors, factors_in, gow, gvw, new, rebuilt,
-    load_sem, send_sem, recv_sem, store_sem,
+    u, x, wv, att, sums, vg, gvw, new, rebuilt,
+    wo, wv_far, scores, feedback, basis,
+    att_t, vg_far, parts, out_stage, in_hop, in_left, in_right,
+    factors, factors_in,
+    load_sem, send_sem, recv_sem,
 ):
     rows, width = u_hbm.shape
     half = rows // 2
@@ -51,10 +58,7 @@
     behind = (lax.rem(s + n_section - 1, n_section), t)
     ahead = (lax.rem(s + 1, n_section), t)
 
-    owner = [place(step, which) for which in (core, 1 - core) for step in (0, 3, 1, 2)]
-
-    def block_of(slot):
-        return pl.ds(pl.multiple_of(owner[slot] * width, 128), width)
+    block_of = blocks(chip, core, width)
 
     lo, hi = pl.ds(0, half), pl.ds(half, half)
 
@@ -135,10 +139,6 @@
     u2lo.wait_recv()
     u6lo = send(u.at[2, lo], u.at[6, lo], sister)
 
-    x1lo = send(x_hbm.at[lo], x.at[1, lo], right)
-    x2hi = send(x_hbm.at[hi], x.at[2, hi], left)
-    x4 = send(x_hbm, x.at[4], sister)
-
     add_u(1)
     add_u(2)
     u5lo.wait_recv()
@@ -147,6 +147,9 @@
     u6lo.wait_recv()
     u6hi.wait_recv()
     add_u(6)
+    x1lo = send(x_hbm.at[lo], x.at[1, lo], right)
+    x2hi = send(x_hbm.at[hi], x.at[2, hi], left)
+    x4 = send(x_hbm, x.at[4], sister)
     u3lo.wait_recv()
     u7lo = send(u.at[3, lo], u.at[7, lo], sister)
     u3hi.wait_recv()
@@ -155,9 +158,6 @@
     u7lo.wait_recv()
     u7hi.wait_recv()
     add_u(7)
-
-    x1hi = send(x_hbm.at[hi], x.at[1, hi], right)
-    x2lo = send(x_hbm.at[lo], x.at[2, lo], left)
 
     for b in range(micro):
         for h in range(heads):
@@ -195,16 +195,8 @@
         term = dot(x[slot], wv[block_of(slot), :])
         sums[...] = term if first else sums[...] + term
 
-    stores = []
-
-    def store(src, dst):
-        copy = pltpu.make_async_copy(src, dst, store_sem.at[len(stores)])
-        copy.start()
-        stores.append(copy)
-
     def grad_value(slot):
         gvw[slot] = dot(x[slot], vg[...], TN).astype(BF16)
-        store(gvw.at[slot], gvw_hbm.at[block_of(slot)])
 
     def take_x(slot, first=False):
         add_x(slot, first)
@@ -212,12 +204,12 @@
 
     got_x.wait()
     take_x(0, True)
+    x4.wait_recv()
+    take_x(4)
 
     x1lo.wait_recv()
-    x3lo = send(x.at[1, lo], x.at[3, lo], right)
     x5lo = send(x.at[1, lo], x.at[5, lo], sister)
     x2hi.wait_recv()
-    x3hi = send(x.at[2, hi], x.at[3, hi], left)
     x6hi = send(x.at[2, hi], x.at[6, hi], sister)
 
     hop_right.wait_recv()
@@ -227,29 +219,18 @@
     out_stage[2, 1] = (parts[3, half:] + in_hop[1].astype(F32)).astype(BF16)
     last_left_hi = send(out_stage.at[2, 1], in_right.at[1], left)
 
-    x4.wait_recv()
-    take_x(4)
-
-    x1hi.wait_recv()
-    x5hi = send(x.at[1, hi], x.at[5, hi], sister)
-    x2lo.wait_recv()
-    x6lo = send(x.at[2, lo], x.at[6, lo], sister)
-    take_x(1)
-    take_x(2)
-    x5lo.wait_recv()
-    x5hi.wait_recv()
-    take_x(5)
-    x6lo.wait_recv()
-    x6hi.wait_recv()
-    take_x(6)
+    x1hi = send(x_hbm.at[hi], x.at[1, hi], right)
+    x2lo = send(x_hbm.at[lo], x.at[2, lo], left)
+    x3lo = send(x.at[1, lo], x.at[3, lo], right)
+    x3hi = send(x.at[2, hi], x.at[3, hi], left)
 
     got_feedback.wait()
     got_basis.wait()
     basis_high, basis_low = halves(basis[...])
     feedback[...] += u[0].astype(F32) + parts[0]
-    last_right_lo.wait_recv()
     last_right_hi.wait_recv()
     last_left_lo.wait_recv()
+    last_right_lo.wait_recv()
     last_left_hi.wait_recv()
     carried = feedback[...] + in_left[...].astype(F32).reshape(rows, width)
     carried = carried + in_right[...].astype(F32).reshape(rows, width)
@@ -258,38 +239,71 @@
     factor_copy = send(factors, factors_in, behind)
     own = factors[...]
     new[...] = carried - (dot(own, basis_high, NT) + dot(own, basis_low, NT))
-    store(new, new_hbm)
+
+    x1hi.wait_recv()
+    x5hi = send(x.at[1, hi], x.at[5, hi], sister)
+    x2lo.wait_recv()
+    x6lo = send(x.at[2, lo], x.at[6, lo], sister)
+    take_x(1)
+    take_x(2)
+
+    factor_copy.wait_recv()
+    arrived = factors_in[...]
+    built = dot(arrived, basis_high, NT) + dot(arrived, basis_low, NT)
+    rebuilt[...] = jnp.where(s == n_section - 1, 0.0, built).astype(BF16)
+
+    x5lo.wait_recv()
+    x5hi.wait_recv()
+    take_x(5)
+    x6lo.wait_recv()
+    x6hi.wait_recv()
+    take_x(6)
 
     x3lo.wait_recv()
     x7lo = send(x.at[3, lo], x.at[7, lo], sister)
     x3hi.wait_recv()
     x7hi = send(x.at[3, hi], x.at[7, hi], sister)
     take_x(3)
-
-    factor_copy.wait_recv()
-    arrived = factors_in[...]
-    built = dot(arrived, basis_high, NT) + dot(arrived, basis_low, NT)
-    rebuilt[...] = jnp.where(s == n_section - 1, 0.0, built).astype(BF16)
-    store(rebuilt, rebuilt_hbm)
-
     x7lo.wait_recv()
     x7hi.wait_recv()
-    take_x(7)
-
+    for copy in sent:
+        copy.wait_send()
+
+
+def finish(
+    micro, heads, u, x, wv, att, sums, vg, gvw, new, rebuilt,
+    gow_hbm, gvw_hbm, new_hbm, rebuilt_hbm, last, gow, attended, store_sem,
+):
+    width = u.shape[2]
+    length = att.shape[1]
+    head = wv.shape[1] // heads
+    t = lax.axis_index("tensor")
+    block_of = blocks(t // 2, lax.rem(t, 2), width)
+    stores = []
+
+    def store(src, dst):
+        copy = pltpu.make_async_copy(src, dst, store_sem.at[len(stores)])
+        copy.start()
+        stores.append(copy)
+
+    for slot in range(7):
+        store(gvw.at[slot], gvw_hbm.at[block_of(slot)])
+    store(new, new_hbm)
+    store(rebuilt, rebuilt_hbm)
+
+    value = sums[...] + dot(x[7], wv[block_of(7), :])
     for b in range(micro):
         for h in range(heads):
-            at_rows, at_columns = pl.ds(b * length, length), pl.ds(h * head, head)
-            value = dot(att[b * heads + h], sums[at_rows, at_columns].astype(BF16))
-            vg_far[at_rows, at_columns] = value.astype(BF16)
-    attended = vg_far[...]
+            at_rows, at_columns = slice(b * length, (b + 1) * length), slice(h * head, (h + 1) * head)
+            mixed = dot(att[b * heads + h], value[at_rows, at_columns].astype(BF16))
+            attended[at_rows, at_columns] = mixed.astype(BF16)
     for slot in range(8):
-        gow[slot] = dot(attended, u[slot], TN).astype(BF16)
+        gow[slot] = dot(attended[...], u[slot], TN).astype(BF16)
         store(gow.at[slot], gow_hbm.at[:, block_of(slot)])
-
+    last[...] = dot(x[7], vg[...], TN).astype(BF16)
+    store(last, gvw_hbm.at[block_of(7)])
     for copy in stores:
         copy.wait()
-    for copy in sent:
-        copy.wait_send()
 
 
 def on_device(n_section, layer_input, upstream, scores, value_weight, out_weight, feedback, basis):
@@ -300,29 +314,29 @@
     rank = basis.shape[1]
     vmem = pltpu.VMEM
     anywhere = pl.BlockSpec(memory_space=pl.ANY)
-    gow, gvw, new, rebuilt = pl.pallas_call(
+    whole = pl.BlockSpec(memory_space=vmem)
+    held = pl.pallas_call(
         functools.partial(body, micro, heads, n_section),
         out_shape=(
-            jax.ShapeDtypeStruct((inner, model), BF16),
-            jax.ShapeDtypeStruct((model, inner), BF16),
-            jax.ShapeDtypeStruct((rows, width), F32),
-            jax.ShapeDtypeStruct((rows, width), BF16),
-        ),
-        in_specs=[anywhere] * 7,
-        out_specs=(anywhere,) * 4,
-        scratch_shapes=[
             vmem((8, rows, width), BF16),
             vmem((8, rows, width), BF16),
             vmem((model, inner), BF16),
+            vmem((micro * heads, length, length), BF16),
+            vmem((rows, inner), F32),
+            vmem((rows, inner), BF16),
+            vmem((8, width, inner), BF16),
+            vmem((rows, width), F32),
+            vmem((rows, width), BF16),
+        ),
+        in_specs=[anywhere] * 7,
+        out_specs=(whole,) * 9,
+        scratch_shapes=[
             vmem((inner, model), BF16),
             vmem((4, width, inner), BF16),
             vmem((micro * heads, length, length), BF16),
             vmem((rows, width), F32),
             vmem((width, rank), F32),
             vmem((micro * heads, length, length), BF16),
-            vmem((micro * heads, length, length), BF16),
-            vmem((rows, inner), F32),
-            vmem((rows, inner), BF16),
             vmem((rows, inner), BF16),
             vmem((4, rows, width), F32),
             vmem((3, 2, half, width), BF16),
@@ -331,27 +345,44 @@
             vmem((2, half, width), BF16),
             vmem((rows, rank), BF16),
             vmem((rows, rank), BF16),
-            vmem((8, inner, width), BF16),
-            vmem((8, width, inner), BF16),
-            vmem((rows, width), F32),
-            vmem((rows, width), BF16),
             pltpu.SemaphoreType.DMA((7,)),
             pltpu.SemaphoreType.DMA((40,)),
             pltpu.SemaphoreType.DMA((40,)),
+        ],
+        compiler_params=pltpu.CompilerParams(
+            collective_id=0, has_side_effects=True, vmem_limit_bytes=40 << 20
+        ),
+    )(*(
+        pltpu.with_memory_space_constraint(value, pltpu.HBM)
+        for value in (
+            layer_input.reshape(rows, width),
+            upstream.reshape(rows, width),
+            scores.reshape(micro * heads, length, length),
+            value_weight[0],
+            out_weight[0],
+            feedback.reshape(rows, width),
+            basis,
+        )
+    ))
+    u, x, *others = held
+    gow, gvw, new, rebuilt = pl.pallas_call(
+        functools.partial(finish, micro, heads),
+        out_shape=(
+            jax.ShapeDtypeStruct((inner, model), BF16),
+            jax.ShapeDtypeStruct((model, inner), BF16),
+            jax.ShapeDtypeStruct((rows, width), F32),
+            jax.ShapeDtypeStruct((rows, width), BF16),
+        ),
+        in_specs=[whole] * 9,
+        out_specs=(anywhere,) * 4,
+        scratch_shapes=[
+            vmem((width, inner), BF16),
+            vmem((8, inner, width), BF16),
+            vmem((rows, inner), BF16),
             pltpu.SemaphoreType.DMA((18,)),
         ],
-        compiler_params=pltpu.CompilerParams(
-            collective_id=0, has_side_effects=True, vmem_limit_bytes=56 << 20
-        ),
-    )(
-        layer_input.reshape(rows, width),
-        upstream.reshape(rows, width),
-        scores.reshape(micro * heads, length, length),
-        value_weight[0],
-        out_weight[0],
-        feedback.reshape(rows, width),
-        basis,
-    )
+        compiler_params=pltpu.CompilerParams(vmem_limit_bytes=16 << 20),
+    )(*(pltpu.with_memory_space_constraint(value, pltpu.VMEM) for value in (u, x, *others)))
     shape = (1, micro, length, width)
     return gow[None], gvw[None], new.reshape(shape), rebuilt.reshape(shape)
 

time: 103 us -> 96.6 us (0.938)
  the two profiles are of different devices: /device:TPU:6 before, /device:TPU:9 now
where the time goes in v2:
time: 96.6 us
  Pallas kernels  95.9 us (99%)
    pallas_call x1, Pallas kernels, on_device(): pl.pallas_call(functools.partial(body, micro, heads, n_section), out_shap...  93 us
    pallas_call x1, Pallas kernels, on_device(): pl.pallas_call(functools.partial(finish, micro, heads), out_shape=(jax.Sh...  2.94 us

profile of v2, /device:TPU:9, one launch (start us, length us, event | category | flops | bytes accessed | tf_op | source)
XLA Modules:
  0.0 96.6 jit_solution(6816058398380235709)
XLA Ops:
  0.6 93.0 %shard_map.102 = (bf16[8,512,384]{2,1,0:T(8,128)(2,1)S(1)}, bf16[8,512,384]{2,1,0:T(8,128)(2,1)S(1)}, bf16[3072,256]{1,0:T(8,128)(2,1)S(1)}, bf16[4,256,256]{2,1...) custom-call(bf16[512,384]{1,0:T(8,128)(2,1)} %bitcast.14, ...), custom_call_target="tpu_custom_call" | custom-call | tf_op jit(solution)/shard_map/pallas_call | solution.py:318
  93.6 2.9 %shard_map.103 = (bf16[256,3072]{1,0:T(8,128)(2,1)}, bf16[3072,256]{1,0:T(8,128)(2,1)}, f32[512,384]{1,0:T(8,128)}, bf16[512,384]{1,0:T(8,128)(2,1)}) custom-call(bf16[8,512,384]{2,1,0:T(8,128)(2,1)S(1)} %get-tuple-element.17.u, bf16[8,512,384]{2,1,0:T(8,128)(2,1)S(1)} %get-tuple-element.18.x, bf16[3072,256]{1,0:T(8,128)(2,1)S(1)} %get-tuple-element.19.wv, ...), custom_call_target="tpu_custom_call" | custom-call | tf_op jit(solution)/shard_map/pallas_call | solution.py:368

commit v3 on v2

v3 whole, which is shorter than its diff:
```python
import functools

import jax
import jax.numpy as jnp
from jax import lax
from jax.experimental import pallas as pl
from jax.experimental.pallas import tpu as pltpu
from jax.sharding import PartitionSpec as P

MESH = pl.DeviceIdType.MESH
NT = (((1,), (1,)), ((), ()))
TN = (((0,), (0,)), ((), ()))
ROW = 8
F32 = jnp.float32
BF16 = jnp.bfloat16


def dot(a, b, dims=(((1,), (0,)), ((), ()))):
    return lax.dot_general(a, b, dims, preferred_element_type=F32)


def halves(value):
    high = value.astype(BF16)
    return high, (value - high.astype(F32)).astype(BF16)


def blocks(chip, core, width):
    owner = [
        lax.rem(chip + step, 4) * 2 + which for which in (core, 1 - core) for step in (0, 3, 1, 2)
    ]
    return lambda slot: pl.ds(pl.multiple_of(owner[slot] * width, 128), width)


def body(
    micro, heads, n_section,
    x_hbm, u_hbm, scores_hbm, wv_hbm, wo_hbm, feedback_hbm, basis_hbm,
    u, x, wv, att, va, vg, gow_first, gvw, new, factors_in, basis,
    wo, wv_far, scores, feedback,
    att_t, ag, vg_far, parts, out_stage, in_hop, in_left, in_right, factors,
    load_sem, send_sem, recv_sem, factor_sem,
):
    rows, width = u_hbm.shape
    length = rows // micro
    quarter = length // 2
    inner = wv_hbm.shape[1]
    head = inner // heads

    s = lax.axis_index("section")
    t = lax.axis_index("tensor")
    chip, core = t // 2, lax.rem(t, 2)

    def place(step, which):
        return lax.rem(chip + step, 4) * 2 + which

    right = (s, place(1, core))
    left = (s, place(3, core))
    sister = (s, place(0, 1 - core))

    row_first, row_last = lax.rem(s, ROW) == 0, lax.rem(s, ROW) == ROW - 1

    def section(step):
        return lax.rem(s + n_section + step, n_section)

    behind = (jnp.where(row_first, section(ROW - 1), section(-1)), t)
    beyond = (section(-ROW), t)
    block_of = blocks(chip, core, width)

    def batch(m):
        return pl.ds(m * length, length)

    def first(m):
        return pl.ds(m * length, quarter)

    def second(m):
        return pl.ds(m * length + quarter, quarter)

    loads = []

    def load(src, dst):
        copy = pltpu.make_async_copy(src, dst, load_sem.at[len(loads)])
        copy.start()
        loads.append(copy)
        return copy

    got_scores = load(scores_hbm, scores)
    got_u = load(u_hbm, u.at[0])
    got_wo = load(wo_hbm, wo)
    got_wv = load(wv_hbm, wv)
    got_x = load(x_hbm, x.at[0])
    got_feedback = load(feedback_hbm, feedback)
    got_basis = load(basis_hbm, basis)

    barrier = pltpu.get_barrier_semaphore()
    peers = (right, left, sister, (jnp.where(row_last, section(ROW), section(1)), t))
    for peer in peers:
        pl.semaphore_signal(barrier, inc=1, device_id=peer, device_id_type=MESH)

    @pl.when(row_last)
    def _():
        pl.semaphore_signal(barrier, inc=1, device_id=(section(1 - ROW), t), device_id_type=MESH)

    pl.semaphore_wait(barrier, len(peers) + row_last.astype(jnp.int32))

    sent = []

    def send(src, dst, device):
        i = len(sent)
        copy = pltpu.make_async_remote_copy(
            src_ref=src, dst_ref=dst, send_sem=send_sem.at[i], recv_sem=recv_sem.at[i],
            device_id=device, device_id_type=MESH,
        )
        copy.start()
        sent.append(copy)
        return copy

    def arrive(*copies):
        for copy in copies:
            copy.wait_recv()

    def spread(src, dst, m):
        return (
            send(src.at[first(m)], dst.at[1, first(m)], right),
            send(src.at[second(m)], dst.at[2, second(m)], left),
            send(src.at[second(m)], dst.at[1, second(m)], right),
            send(src.at[first(m)], dst.at[2, first(m)], left),
        )

    def relay(dst, m, copies):
        arrive(copies[0])
        onward = send(dst.at[1, first(m)], dst.at[3, first(m)], right)
        arrive(copies[1])
        return onward, send(dst.at[2, second(m)], dst.at[3, second(m)], left)

    def share(dst, slot, rows_):
        return send(dst.at[slot, rows_], dst.at[slot + 4, rows_], sister)

    u_out = [spread(u_hbm, u, 0)]
    u_own = send(u_hbm, u.at[4], sister)
    far = []
    for step in range(4):
        block = pl.ds(pl.multiple_of(place(step, 1 - core) * width, 128), width)
        far.append(send(wv_hbm.at[block], wv_far.at[step], sister))

    got_scores.wait()
    query = lax.broadcasted_iota(jnp.int32, (length, length), 0)
    key = lax.broadcasted_iota(jnp.int32, (length, length), 1)
    causal = key <= query
    for i in range(micro * heads):
        raised = jnp.where(causal, scores[i].astype(F32), -1e30)
        largest = jnp.max(raised, axis=-1, keepdims=True)
        powers = jnp.where(causal, jnp.exp(raised - largest), 0.0)
        probs = powers / jnp.sum(powers, axis=-1, keepdims=True)
        att[i] = probs.astype(BF16)
        att_t[i] = probs.T.astype(BF16)

    def add_u(m, *slots):
        total = ag[batch(m)]
        for slot in slots:
            total = total + dot(u[slot, batch(m)], wo[:, block_of(slot)], NT)
        ag[batch(m)] = total

    got_u.wait()
    got_wo.wait()
    ag[...] = dot(u[0], wo[:, block_of(0)], NT)

    def value_grad(m):
        for h in range(heads):
            columns = pl.ds(h * head, head)
            grad = dot(att_t[m * heads + h], ag[batch(m), columns].astype(BF16))
            vg[batch(m), columns] = grad.astype(BF16)
        return send(vg.at[batch(m)], vg_far.at[batch(m)], sister)

    def partial(m, step):
        block = pl.ds(pl.multiple_of(place(step, core) * width, 128), width)
        near = dot(vg[batch(m)], wv[block, :], NT)
        return near + dot(vg_far[batch(m)], wv_far[step], NT)

    def begin_sums(m):
        out_stage[0, batch(m)] = partial(m, 2).astype(BF16)
        hops = (
            send(out_stage.at[0, first(m)], in_hop.at[first(m)], right),
            send(out_stage.at[0, second(m)], in_hop.at[second(m)], left),
        )
        parts[1, batch(m)] = partial(m, 1)
        out_stage[1, second(m)] = parts[1, second(m)].astype(BF16)
        ends = [send(out_stage.at[1, second(m)], in_left.at[second(m)], right)]
        parts[2, batch(m)] = partial(m, 3)
        out_stage[2, first(m)] = parts[2, first(m)].astype(BF16)
        ends.append(send(out_stage.at[2, first(m)], in_right.at[first(m)], left))
        parts[0, batch(m)] = partial(m, 0)
        return hops, ends

    def end_sums(m, hops, ends):
        arrive(hops[0])
        out_stage[1, first(m)] = (parts[1, first(m)] + in_hop[first(m)].astype(F32)).astype(BF16)
        ends.append(send(out_stage.at[1, first(m)], in_left.at[first(m)], right))
        arrive(hops[1])
        out_stage[2, second(m)] = (parts[2, second(m)] + in_hop[second(m)].astype(F32)).astype(BF16)
        ends.append(send(out_stage.at[2, second(m)], in_right.at[second(m)], left))

    def gather_u(m, copies, onward):
        arrive(*copies[2:])
        shared = share(u, 1, batch(m)), share(u, 2, batch(m))
        add_u(m, 1, 2)
        arrive(*shared)
        add_u(m, 5, 6)
        arrive(*onward)
        shared = share(u, 3, batch(m))
        add_u(m, 3)
        arrive(shared)
        add_u(m, 7)
        return value_grad(m)

    u_on = [relay(u, 0, u_out[0])]
    u_out.append(spread(u_hbm, u, 1))
    arrive(u_own)
    ag[...] += dot(u[4], wo[:, block_of(4)], NT)
    vg_copy = gather_u(0, u_out[0], u_on[0])
    u_on.append(relay(u, 1, u_out[1]))
    got_wv.wait()
    arrive(vg_copy, *far)
    hops0, ends0 = begin_sums(0)
    x_out = [spread(x_hbm, x, 0)]
    x_own = send(x_hbm, x.at[4], sister)
    vg_copy = gather_u(1, u_out[1], u_on[1])
    end_sums(0, hops0, ends0)
    arrive(vg_copy)
    hops1, ends1 = begin_sums(1)

    def add_x(m, *slots):
        total = va[batch(m)]
        for slot in slots:
            total = total + dot(x[slot, batch(m)], wv[block_of(slot), :])
        va[batch(m)] = total

    def grad_value(slot):
        gvw[slot] = dot(x[slot], vg[...], TN).astype(BF16)

    x_on = [relay(x, 0, x_out[0])]
    got_x.wait()
    va[...] = dot(x[0], wv[block_of(0), :])
    grad_value(0)
    arrive(x_own)
    va[...] += dot(x[4], wv[block_of(4), :])
    grad_value(4)
    arrive(*x_out[0][2:])
    shared = share(x, 1, batch(0)), share(x, 2, batch(0))
    add_x(0, 1, 2)
    arrive(*shared)
    add_x(0, 5, 6)
    got_feedback.wait()
    got_basis.wait()
    basis_high, basis_low = halves(basis[...])
    slot = row_first.astype(jnp.int32)

    def compress(m, ends):
        arrive(*ends)
        carried = feedback[batch(m)] + u[0, batch(m)].astype(F32) + parts[0, batch(m)]
        carried = carried + in_left[batch(m)].astype(F32) + in_right[batch(m)].astype(F32)
        high, low = halves(carried)
        found = dot(high, basis_high) + dot(low, basis_high) + dot(high, basis_low)
        own = found.astype(BF16)
        factors[batch(m)] = own
        copy = pltpu.make_async_remote_copy(
            src_ref=factors.at[batch(m)], dst_ref=factors_in.at[slot, batch(m)],
            send_sem=factor_sem.at[0, m], recv_sem=factor_sem.at[2 + slot, m],
            device_id=behind, device_id_type=MESH,
        )
        copy.start()
        new[batch(m)] = carried - (dot(own, basis_high, NT) + dot(own, basis_low, NT))
        return copy

    def passing(m, which):
        return pltpu.make_async_remote_copy(
            src_ref=factors_in.at[1, batch(m)], dst_ref=factors_in.at[which, batch(m)],
            send_sem=factor_sem.at[1, m], recv_sem=factor_sem.at[2 + which, m],
            device_id=beyond, device_id_type=MESH,
        )

    def pass_on(m):
        @pl.when(row_last)
        def _():
            passing(m, 1).wait_recv()
            passing(m, 0).start()

    factor_copies = [compress(0, ends0)]
    end_sums(1, hops1, ends1)
    x_out.append(spread(x_hbm, x, 1))
    pass_on(0)
    factor_copies.append(compress(1, ends1))

    arrive(*x_on[0])
    shared = share(x, 3, batch(0))
    add_x(0, 3)
    arrive(shared)
    add_x(0, 7)
    x_on.append(relay(x, 1, x_out[1]))
    mixed = attended(0, heads, va, att)
    for slot in range(8):
        gow_first[slot] = dot(mixed, u[slot, batch(0)])

    arrive(*x_out[1][2:])
    shared = share(x, 1, batch(1)), share(x, 2, batch(1))
    add_x(1, 1, 2)
    grad_value(1)
    grad_value(2)
    arrive(*shared)
    add_x(1, 5, 6)
    grad_value(5)
    grad_value(6)

    pass_on(1)
    arrive(x_on[1][0])
    last = [share(x, 3, first(1))]
    arrive(x_on[1][1])
    last.append(share(x, 3, second(1)))
    add_x(1, 3)
    grad_value(3)
    arrive(*last)
    for m in range(micro):
        passing(m, 0).wait_recv()
        factor_copies[m].wait_send()

    @pl.when(row_last)
    def _():
        for m in range(micro):
            passing(m, 0).wait_send()

    for copy in sent:
        copy.wait_send()


def attended(m, heads, va, att):
    length = att.shape[1]
    head = va.shape[1] // heads
    found = []
    for h in range(heads):
        value = va[pl.ds(m * length, length), pl.ds(h * head, head)]
        found.append(dot(value.T.astype(BF16), att[m * heads + h], NT).astype(BF16))
    return jnp.concatenate(found, axis=0)


def finish(
    micro, heads, n_section, u, x, wv, att, va, vg, gow_first, gvw, new, factors_in, basis,
    gow_hbm, gvw_hbm, new_hbm, rebuilt_hbm, last, gow, total, rebuilt, store_sem,
):
    width = u.shape[2]
    length = att.shape[1]
    s = lax.axis_index("section")
    t = lax.axis_index("tensor")
    block_of = blocks(t // 2, lax.rem(t, 2), width)
    stores = []

    def store(src, dst):
        copy = pltpu.make_async_copy(src, dst, store_sem.at[len(stores)])
        copy.start()
        stores.append(copy)

    for slot in range(7):
        store(gvw.at[slot], gvw_hbm.at[block_of(slot)])
    store(new, new_hbm)

    rows = pl.ds((micro - 1) * length, length)
    total[rows] = va[rows] + dot(x[7, rows], wv[block_of(7), :])
    mixed = attended(micro - 1, heads, total, att)
    for slot in range(8):
        gow[slot] = (gow_first[slot] + dot(mixed, u[slot, rows])).astype(BF16)
        store(gow.at[slot], gow_hbm.at[:, block_of(slot)])
    basis_high, basis_low = halves(basis[...])
    arrived = factors_in[0]
    built = dot(arrived, basis_high, NT) + dot(arrived, basis_low, NT)
    rebuilt[...] = jnp.where(s == n_section - 1, 0.0, built).astype(BF16)
    store(rebuilt, rebuilt_hbm)
    last[...] = dot(x[7], vg[...], TN).astype(BF16)
    store(last, gvw_hbm.at[block_of(7)])
    for copy in stores:
        copy.wait()


def on_device(n_section, layer_input, upstream, scores, value_weight, out_weight, feedback, basis):
    _, micro, length, width = layer_input.shape
    rows = micro * length
    heads = scores.shape[2]
    model, inner = value_weight.shape[1:]
    rank = basis.shape[1]
    vmem = pltpu.VMEM
    anywhere = pl.BlockSpec(memory_space=pl.ANY)
    whole = pl.BlockSpec(memory_space=vmem)
    held = pl.pallas_call(
        functools.partial(body, micro, heads, n_section),
        out_shape=(
            vmem((8, rows, width), BF16),
            vmem((8, rows, width), BF16),
            vmem((model, inner), BF16),
            vmem((micro * heads, length, length), BF16),
            vmem((rows, inner), F32),
            vmem((rows, inner), BF16),
            vmem((8, inner, width), F32),
            vmem((8, width, inner), BF16),
            vmem((rows, width), F32),
            vmem((2, rows, rank), BF16),
            vmem((width, rank), F32),
        ),
        in_specs=[anywhere] * 7,
        out_specs=(whole,) * 11,
        scratch_shapes=[
            vmem((inner, model), BF16),
            vmem((4, width, inner), BF16),
            vmem((micro * heads, length, length), BF16),
            vmem((rows, width), F32),
            vmem((micro * heads, length, length), BF16),
            vmem((rows, inner), F32),
            vmem((rows, inner), BF16),
            vmem((3, rows, width), F32),
            vmem((3, rows, width), BF16),
            vmem((rows, width), BF16),
            vmem((rows, width), BF16),
            vmem((rows, width), BF16),
            vmem((rows, rank), BF16),
            pltpu.SemaphoreType.DMA((7,)),
            pltpu.SemaphoreType.DMA((80,)),
            pltpu.SemaphoreType.DMA((80,)),
            pltpu.SemaphoreType.DMA((4, micro)),
        ],
        compiler_params=pltpu.CompilerParams(
            collective_id=0, has_side_effects=True, vmem_limit_bytes=40 << 20
        ),
    )(*(
        pltpu.with_memory_space_constraint(value, pltpu.HBM)
        for value in (
            layer_input.reshape(rows, width),
            upstream.reshape(rows, width),
            scores.reshape(micro * heads, length, length),
            value_weight[0],
            out_weight[0],
            feedback.reshape(rows, width),
            basis,
        )
    ))
    gow, gvw, new, rebuilt = pl.pallas_call(
        functools.partial(finish, micro, heads, n_section),
        out_shape=(
            jax.ShapeDtypeStruct((inner, model), BF16),
            jax.ShapeDtypeStruct((model, inner), BF16),
            jax.ShapeDtypeStruct((rows, width), F32),
            jax.ShapeDtypeStruct((rows, width), BF16),
        ),
        in_specs=[whole] * 11,
        out_specs=(anywhere,) * 4,
        scratch_shapes=[
            vmem((width, inner), BF16),
            vmem((8, inner, width), BF16),
            vmem((rows, inner), F32),
            vmem((rows, width), BF16),
            pltpu.SemaphoreType.DMA((18,)),
        ],
        compiler_params=pltpu.CompilerParams(vmem_limit_bytes=16 << 20),
    )(*(pltpu.with_memory_space_constraint(value, pltpu.VMEM) for value in held))
    shape = (1, micro, length, width)
    return gow[None], gvw[None], new.reshape(shape), rebuilt.reshape(shape)


def solution(mesh):
    in_specs = (
        P("section", None, None, "tensor"),
        P("section", None, None, "tensor"),
        P("section", None, "tensor", None, None),
        P("section", None, "tensor"),
        P("section", "tensor", None),
        P("section", None, None, "tensor"),
        P("tensor", None),
    )
    out_specs = (
        P("section", "tensor", None),
        P("section", None, "tensor"),
        P("section", None, None, "tensor"),
        P("section", None, None, "tensor"),
    )
    return jax.shard_map(
        functools.partial(on_device, mesh.shape["section"]),
        mesh=mesh, in_specs=in_specs, out_specs=out_specs, check_vma=False,
    )
```

time: 96.6 us -> 95.8 us (level)
  the two profiles are of different devices: /device:TPU:9 before, /device:TPU:6 now
where the time goes in v3:
time: 95.8 us; the launch traced here: 94.1 us
  Pallas kernels  93.4 us (97%)
    pallas_call x1, Pallas kernels, on_device(): pl.pallas_call(functools.partial(body, micro, heads, n_section), out_shap...  91 us
    pallas_call x1, Pallas kernels, on_device(): pl.pallas_call(functools.partial(finish, micro, heads, n_section), out_sh...  2.44 us

profile of v3, /device:TPU:6, one launch (start us, length us, event | category | flops | bytes accessed | tf_op | source)
XLA Modules:
  0.0 94.1 jit_solution(7240774403872419145)
XLA Ops:
  0.6 91.0 %shard_map.102 = (bf16[8,512,384]{2,1,0:T(8,128)(2,1)S(1)}, bf16[8,512,384]{2,1,0:T(8,128)(2,1)S(1)}, bf16[3072,256]{1,0:T(8,128)(2,1)S(1)}, bf16[4,256,256]{2,1...) custom-call(bf16[512,384]{1,0:T(8,128)(2,1)} %bitcast.14, ...), custom_call_target="tpu_custom_call" | custom-call | tf_op jit(solution)/shard_map/pallas_call | solution.py:389
  91.6 2.4 %shard_map.103 = (bf16[256,3072]{1,0:T(8,128)(2,1)}, bf16[3072,256]{1,0:T(8,128)(2,1)}, f32[512,384]{1,0:T(8,128)}, bf16[512,384]{1,0:T(8,128)(2,1)}) custom-call(bf16[8,512,384]{2,1,0:T(8,128)(2,1)S(1)} %get-tuple-element.19.u, bf16[8,512,384]{2,1,0:T(8,128)(2,1)S(1)} %get-tuple-element.20.x, bf16[3072,256]{1,0:T(8,128)(2,1)S(1)} %get-tuple-element.21.wv, ...), custom_call_target="tpu_custom_call" | custom-call | tf_op jit(solution)/shard_map/pallas_call | solution.py:440

commit v4 on v3

--- a/solution.py
+++ b/solution.py
@@ -37,7 +37,7 @@
     u, x, wv, att, va, vg, gow_first, gvw, new, factors_in, basis,
     wo, wv_far, scores, feedback,
     att_t, ag, vg_far, parts, out_stage, in_hop, in_left, in_right, factors,
-    load_sem, send_sem, recv_sem, factor_sem,
+    load_sem, send_sem, recv_sem, begun_sem,
 ):
     rows, width = u_hbm.shape
     length = rows // micro
@@ -59,10 +59,8 @@
     row_first, row_last = lax.rem(s, ROW) == 0, lax.rem(s, ROW) == ROW - 1
 
     def section(step):
-        return lax.rem(s + n_section + step, n_section)
-
-    behind = (jnp.where(row_first, section(ROW - 1), section(-1)), t)
-    beyond = (section(-ROW), t)
+        return lax.rem(s + n_section + step, n_section), t
+
     block_of = blocks(chip, core, width)
 
     def batch(m):
@@ -91,15 +89,22 @@
     got_basis = load(basis_hbm, basis)
 
     barrier = pltpu.get_barrier_semaphore()
-    peers = (right, left, sister, (jnp.where(row_last, section(ROW), section(1)), t))
-    for peer in peers:
+    for peer in (right, left, sister):
         pl.semaphore_signal(barrier, inc=1, device_id=peer, device_id_type=MESH)
+
+    @pl.when(row_first)
+    def _():
+        pl.semaphore_signal(barrier, inc=1, device_id=section(ROW - 1), device_id_type=MESH)
+
+    pl.semaphore_signal(
+        barrier, inc=1, device_id=(jnp.where(row_last, section(ROW)[0], section(1)[0]), t),
+        device_id_type=MESH,
+    )
+    pl.semaphore_wait(barrier, 4 + row_last.astype(jnp.int32) * 2 - row_first.astype(jnp.int32))
 
     @pl.when(row_last)
     def _():
-        pl.semaphore_signal(barrier, inc=1, device_id=(section(1 - ROW), t), device_id_type=MESH)
-
-    pl.semaphore_wait(barrier, len(peers) + row_last.astype(jnp.int32))
+        pl.semaphore_signal(begun_sem, inc=1, device_id=section(1 - ROW), device_id_type=MESH)
 
     sent = []
 
@@ -251,7 +256,6 @@
     got_feedback.wait()
     got_basis.wait()
     basis_high, basis_low = halves(basis[...])
-    slot = row_first.astype(jnp.int32)
 
     def compress(m, ends):
         arrive(*ends)
@@ -261,33 +265,12 @@
         found = dot(high, basis_high) + dot(low, basis_high) + dot(high, basis_low)
         own = found.astype(BF16)
         factors[batch(m)] = own
-        copy = pltpu.make_async_remote_copy(
-            src_ref=factors.at[batch(m)], dst_ref=factors_in.at[slot, batch(m)],
-            send_sem=factor_sem.at[0, m], recv_sem=factor_sem.at[2 + slot, m],
-            device_id=behind, device_id_type=MESH,
-        )
-        copy.start()
         new[batch(m)] = carried - (dot(own, basis_high, NT) + dot(own, basis_low, NT))
-        return copy
-
-    def passing(m, which):
-        return pltpu.make_async_remote_copy(
-            src_ref=factors_in.at[1, batch(m)], dst_ref=factors_in.at[which, batch(m)],
-            send_sem=factor_sem.at[1, m], recv_sem=factor_sem.at[2 + which, m],
-            device_id=beyond, device_id_type=MESH,
-        )
-
-    def pass_on(m):
-        @pl.when(row_last)
-        def _():
-            passing(m, 1).wait_recv()
-            passing(m, 0).start()
-
-    factor_copies = [compress(0, ends0)]
+
+    compress(0, ends0)
     end_sums(1, hops1, ends1)
     x_out.append(spread(x_hbm, x, 1))
-    pass_on(0)
-    factor_copies.append(compress(1, ends1))
+    compress(1, ends1)
 
     arrive(*x_on[0])
     shared = share(x, 3, batch(0))
@@ -295,6 +278,12 @@
     arrive(shared)
     add_x(0, 7)
     x_on.append(relay(x, 1, x_out[1]))
+
+    @pl.when(row_first)
+    def _():
+        pl.semaphore_wait(begun_sem, 1)
+
+    factor_copy = send(factors, factors_in, section(-1))
     mixed = attended(0, heads, va, att)
     for slot in range(8):
         gow_first[slot] = dot(mixed, u[slot, batch(0)])
@@ -309,23 +298,13 @@
     grad_value(5)
     grad_value(6)
 
-    pass_on(1)
     arrive(x_on[1][0])
     last = [share(x, 3, first(1))]
     arrive(x_on[1][1])
     last.append(share(x, 3, second(1)))
     add_x(1, 3)
     grad_value(3)
-    arrive(*last)
-    for m in range(micro):
-        passing(m, 0).wait_recv()
-        factor_copies[m].wait_send()
-
-    @pl.when(row_last)
-    def _():
-        for m in range(micro):
-            passing(m, 0).wait_send()
-
+    arrive(factor_copy, *last)
     for copy in sent:
         copy.wait_send()
 
@@ -367,7 +346,7 @@
         gow[slot] = (gow_first[slot] + dot(mixed, u[slot, rows])).astype(BF16)
         store(gow.at[slot], gow_hbm.at[:, block_of(slot)])
     basis_high, basis_low = halves(basis[...])
-    arrived = factors_in[0]
+    arrived = factors_in[...]
     built = dot(arrived, basis_high, NT) + dot(arrived, basis_low, NT)
     rebuilt[...] = jnp.where(s == n_section - 1, 0.0, built).astype(BF16)
     store(rebuilt, rebuilt_hbm)
@@ -398,7 +377,7 @@
             vmem((8, inner, width), F32),
             vmem((8, width, inner), BF16),
             vmem((rows, width), F32),
-            vmem((2, rows, rank), BF16),
+            vmem((rows, rank), BF16),
             vmem((width, rank), F32),
         ),
         in_specs=[anywhere] * 7,
@@ -420,7 +399,7 @@
             pltpu.SemaphoreType.DMA((7,)),
             pltpu.SemaphoreType.DMA((80,)),
             pltpu.SemaphoreType.DMA((80,)),
-            pltpu.SemaphoreType.DMA((4, micro)),
+            pltpu.SemaphoreType.REGULAR,
         ],
         compiler_params=pltpu.CompilerParams(
             collective_id=0, has_side_effects=True, vmem_limit_bytes=40 << 20

time: 95.8 us -> 94.2 us (0.983); the launches traced: 94.1 us -> 93.5 us
  no operation moved by 1% of the time
where the time goes in v4:
time: 94.2 us; the launch traced here: 93.5 us
  Pallas kernels  92.9 us (99%)
    pallas_call x1, Pallas kernels, on_device(): pl.pallas_call(functools.partial(body, micro, heads, n_section), out_shap...  90.4 us
    pallas_call x1, Pallas kernels, on_device(): pl.pallas_call(functools.partial(finish, micro, heads, n_section), out_sh...  2.44 us

profile of v4, /device:TPU:6, one launch (start us, length us, event | category | flops | bytes accessed | tf_op | source)
XLA Modules:
  0.0 93.5 jit_solution(3784656398329033999)
XLA Ops:
  0.6 90.4 %shard_map.102 = (bf16[8,512,384]{2,1,0:T(8,128)(2,1)S(1)}, bf16[8,512,384]{2,1,0:T(8,128)(2,1)S(1)}, bf16[3072,256]{1,0:T(8,128)(2,1)S(1)}, bf16[4,256,256]{2,1...) custom-call(bf16[512,384]{1,0:T(8,128)(2,1)} %bitcast.14, ...), custom_call_target="tpu_custom_call" | custom-call | tf_op jit(solution)/shard_map/pallas_call | solution.py:368
  91.1 2.4 %shard_map.103 = (bf16[256,3072]{1,0:T(8,128)(2,1)}, bf16[3072,256]{1,0:T(8,128)(2,1)}, f32[512,384]{1,0:T(8,128)}, bf16[512,384]{1,0:T(8,128)(2,1)}) custom-call(bf16[8,512,384]{2,1,0:T(8,128)(2,1)S(1)} %get-tuple-element.19.u, bf16[8,512,384]{2,1,0:T(8,128)(2,1)S(1)} %get-tuple-element.20.x, bf16[3072,256]{1,0:T(8,128)(2,1)S(1)} %get-tuple-element.21.wv, ...), custom_call_target="tpu_custom_call" | custom-call | tf_op jit(solution)/shard_map/pallas_call | solution.py:419

commit v5 on v4

--- a/solution.py
+++ b/solution.py
@@ -122,13 +122,20 @@
         for copy in copies:
             copy.wait_recv()
 
-    def spread(src, dst, m):
+    def spread_first(src, dst, m):
         return (
             send(src.at[first(m)], dst.at[1, first(m)], right),
             send(src.at[second(m)], dst.at[2, second(m)], left),
+        )
+
+    def spread_second(src, dst, m):
+        return (
             send(src.at[second(m)], dst.at[1, second(m)], right),
             send(src.at[first(m)], dst.at[2, first(m)], left),
         )
+
+    def spread(src, dst, m):
+        return spread_first(src, dst, m) + spread_second(src, dst, m)
 
     def relay(dst, m, copies):
         arrive(copies[0])
@@ -146,6 +153,7 @@
         block = pl.ds(pl.multiple_of(place(step, 1 - core) * width, 128), width)
         far.append(send(wv_hbm.at[block], wv_far.at[step], sister))
 
+    u_out.append(spread_first(u_hbm, u, 1))
     got_scores.wait()
     query = lax.broadcasted_iota(jnp.int32, (length, length), 0)
     key = lax.broadcasted_iota(jnp.int32, (length, length), 1)
@@ -217,21 +225,20 @@
         return value_grad(m)
 
     u_on = [relay(u, 0, u_out[0])]
-    u_out.append(spread(u_hbm, u, 1))
+    u_out[1] += spread_second(u_hbm, u, 1)
     arrive(u_own)
     ag[...] += dot(u[4], wo[:, block_of(4)], NT)
+    u_on.append(relay(u, 1, u_out[1]))
+    x_out = [spread(x_hbm, x, 0)]
+    x_own = send(x_hbm, x.at[4], sister)
     vg_copy = gather_u(0, u_out[0], u_on[0])
-    u_on.append(relay(u, 1, u_out[1]))
     got_wv.wait()
     arrive(vg_copy, *far)
     hops0, ends0 = begin_sums(0)
-    x_out = [spread(x_hbm, x, 0)]
-    x_own = send(x_hbm, x.at[4], sister)
     vg_copy = gather_u(1, u_out[1], u_on[1])
-    end_sums(0, hops0, ends0)
     arrive(vg_copy)
     hops1, ends1 = begin_sums(1)
-
+    end_sums(0, hops0, ends0)
     def add_x(m, *slots):
         total = va[batch(m)]
         for slot in slots:
@@ -241,7 +248,9 @@
     def grad_value(slot):
         gvw[slot] = dot(x[slot], vg[...], TN).astype(BF16)
 
+    end_sums(1, hops1, ends1)
     x_on = [relay(x, 0, x_out[0])]
+    x_out.append(spread(x_hbm, x, 1))
     got_x.wait()
     va[...] = dot(x[0], wv[block_of(0), :])
     grad_value(0)
@@ -249,9 +258,9 @@
     va[...] += dot(x[4], wv[block_of(4), :])
     grad_value(4)
     arrive(*x_out[0][2:])
-    shared = share(x, 1, batch(0)), share(x, 2, batch(0))
+    shared0 = share(x, 1, batch(0)), share(x, 2, batch(0))
     add_x(0, 1, 2)
-    arrive(*shared)
+    arrive(*shared0)
     add_x(0, 5, 6)
     got_feedback.wait()
     got_basis.wait()
@@ -268,14 +277,11 @@
         new[batch(m)] = carried - (dot(own, basis_high, NT) + dot(own, basis_low, NT))
 
     compress(0, ends0)
-    end_sums(1, hops1, ends1)
-    x_out.append(spread(x_hbm, x, 1))
     compress(1, ends1)
-
     arrive(*x_on[0])
-    shared = share(x, 3, batch(0))
+    shared3 = share(x, 3, batch(0))
     add_x(0, 3)
-    arrive(shared)
+    arrive(shared3)
     add_x(0, 7)
     x_on.append(relay(x, 1, x_out[1]))
 
@@ -287,17 +293,15 @@
     mixed = attended(0, heads, va, att)
     for slot in range(8):
         gow_first[slot] = dot(mixed, u[slot, batch(0)])
-
     arrive(*x_out[1][2:])
-    shared = share(x, 1, batch(1)), share(x, 2, batch(1))
+    shared1 = share(x, 1, batch(1)), share(x, 2, batch(1))
     add_x(1, 1, 2)
     grad_value(1)
     grad_value(2)
-    arrive(*shared)
+    arrive(*shared1)
     add_x(1, 5, 6)
     grad_value(5)
     grad_value(6)
-
     arrive(x_on[1][0])
     last = [share(x, 3, first(1))]
     arrive(x_on[1][1])

time: 94.2 us -> 92.2 us (0.979)
  Pallas kernels: 92.9 us -> 91.5 us
    pallas_call x1, Pallas kernels: 90.4 us -> 89 us  [on_device(): pl.pallas_call(functools.partial(body, micro, heads, n_section), out_shap...]
where the time goes in v5:
time: 92.2 us; the launch traced here: 92.1 us
  Pallas kernels  91.5 us (99%)
    pallas_call x1, Pallas kernels, on_device(): pl.pallas_call(functools.partial(body, micro, heads, n_section), out_shap...  89 us
    pallas_call x1, Pallas kernels, on_device(): pl.pallas_call(functools.partial(finish, micro, heads, n_section), out_sh...  2.44 us

profile of v5, /device:TPU:6, one launch (start us, length us, event | category | flops | bytes accessed | tf_op | source)
XLA Modules:
  0.0 92.1 jit_solution(4036051534434357389)
XLA Ops:
  0.6 89.0 %shard_map.102 = (bf16[8,512,384]{2,1,0:T(8,128)(2,1)S(1)}, bf16[8,512,384]{2,1,0:T(8,128)(2,1)S(1)}, bf16[3072,256]{1,0:T(8,128)(2,1)S(1)}, bf16[4,256,256]{2,1...) custom-call(bf16[512,384]{1,0:T(8,128)(2,1)} %bitcast.14, ...), custom_call_target="tpu_custom_call" | custom-call | tf_op jit(solution)/shard_map/pallas_call | solution.py:372
  89.7 2.4 %shard_map.103 = (bf16[256,3072]{1,0:T(8,128)(2,1)}, bf16[3072,256]{1,0:T(8,128)(2,1)}, f32[512,384]{1,0:T(8,128)}, bf16[512,384]{1,0:T(8,128)(2,1)}) custom-call(bf16[8,512,384]{2,1,0:T(8,128)(2,1)S(1)} %get-tuple-element.19.u, bf16[8,512,384]{2,1,0:T(8,128)(2,1)S(1)} %get-tuple-element.20.x, bf16[3072,256]{1,0:T(8,128)(2,1)S(1)} %get-tuple-element.21.wv, ...), custom_call_target="tpu_custom_call" | custom-call | tf_op jit(solution)/shard_map/pallas_call | solution.py:423

commit v6 on v5

--- a/solution.py
+++ b/solution.py
@@ -278,18 +278,18 @@
 
     compress(0, ends0)
     compress(1, ends1)
+    x_on.append(relay(x, 1, x_out[1]))
+
+    @pl.when(row_first)
+    def _():
+        pl.semaphore_wait(begun_sem, 1)
+
+    factor_copy = send(factors, factors_in, section(-1))
     arrive(*x_on[0])
     shared3 = share(x, 3, batch(0))
     add_x(0, 3)
     arrive(shared3)
     add_x(0, 7)
-    x_on.append(relay(x, 1, x_out[1]))
-
-    @pl.when(row_first)
-    def _():
-        pl.semaphore_wait(begun_sem, 1)
-
-    factor_copy = send(factors, factors_in, section(-1))
     mixed = attended(0, heads, va, att)
     for slot in range(8):
         gow_first[slot] = dot(mixed, u[slot, batch(0)])

time: 92.2 us -> 92.2 us (level)
  no operation moved by 1% of the time
where the time goes in v6:
time: 92.2 us; the launch traced here: 92.1 us
  Pallas kernels  91.5 us (99%)
    pallas_call x1, Pallas kernels, on_device(): pl.pallas_call(functools.partial(body, micro, heads, n_section), out_shap...  89 us
    pallas_call x1, Pallas kernels, on_device(): pl.pallas_call(functools.partial(finish, micro, heads, n_section), out_sh...  2.44 us

profile of v6, /device:TPU:6, one launch (start us, length us, event | category | flops | bytes accessed | tf_op | source)
XLA Modules:
  0.0 92.1 jit_solution(5662562764413284186)
XLA Ops:
  0.6 89.0 %shard_map.102 = (bf16[8,512,384]{2,1,0:T(8,128)(2,1)S(1)}, bf16[8,512,384]{2,1,0:T(8,128)(2,1)S(1)}, bf16[3072,256]{1,0:T(8,128)(2,1)S(1)}, bf16[4,256,256]{2,1...) custom-call(bf16[512,384]{1,0:T(8,128)(2,1)} %bitcast.14, ...), custom_call_target="tpu_custom_call" | custom-call | tf_op jit(solution)/shard_map/pallas_call | solution.py:372
  89.7 2.4 %shard_map.103 = (bf16[256,3072]{1,0:T(8,128)(2,1)}, bf16[3072,256]{1,0:T(8,128)(2,1)}, f32[512,384]{1,0:T(8,128)}, bf16[512,384]{1,0:T(8,128)(2,1)}) custom-call(bf16[8,512,384]{2,1,0:T(8,128)(2,1)S(1)} %get-tuple-element.19.u, bf16[8,512,384]{2,1,0:T(8,128)(2,1)S(1)} %get-tuple-element.20.x, bf16[3072,256]{1,0:T(8,128)(2,1)S(1)} %get-tuple-element.21.wv, ...), custom_call_target="tpu_custom_call" | custom-call | tf_op jit(solution)/shard_map/pallas_call | solution.py:423
